TPU v7x, 512 devices: a whole 4x4x16 slice. The times are simulated.
512 devices in a mesh: row: 32 (over y, x, core), col: 16 (over z).
Axes of the slice: x: 4, y: 4, z: 16, core: 2. Of those that a mesh axis runs over, the one named last changes fastest.
Arguments:
- trailing: float32 [16384, 16384], P('row', 'col'), may hold values from -6 to 6
- panel: float32 [16384, 256], P('row', 'col'), may hold values from -6 to 6
- lower_inverse: float32 [256, 256], replicated, may hold values from -1 to 1, as said below
Outputs:
- updated: float32 [16384, 16384], P('row', 'col')
Inputs may be any that keep to these rules, and one draw needn't show every extreme that they name: `lower_inverse`: lower triangular with a positive diagonal.
All inputs are finite; a program needn't handle non-finite values.
Results may differ from a plain program's by a relative error of at most 0.000075.
Values sent between devices are 32-bit elements; how exact they have to be, the bound alone decides.
A program may use at most 64 MiB of HBM per device.

v0:
```python
import jax
import jax.numpy as jnp
from jax import lax
from jax.sharding import PartitionSpec as P


def from_root(block, axis, source):
    block = jnp.where(lax.axis_index(axis) == source, block, jnp.zeros_like(block))
    return lax.psum(block, axis)


def body(trailing, panel, lower_inverse):
    rows_here = panel.shape[0]
    panel_width = lower_inverse.shape[0]
    grid_col = lax.axis_index("col")
    gathered = lax.all_gather(panel, "col", axis=1, tiled=True)
    factor = jnp.dot(
        gathered,
        lower_inverse.T,
        precision=lax.Precision.HIGHEST,
        preferred_element_type=jnp.float32,
    )
    halfway = lax.axis_size("col")
    lower_rows = from_root(factor, "row", grid_col)
    upper_rows = from_root(factor, "row", grid_col + halfway)
    block_count = rows_here // panel_width
    column_factor = jnp.stack(
        [
            lower_rows.reshape(block_count, panel_width, panel_width),
            upper_rows.reshape(block_count, panel_width, panel_width),
        ],
        axis=1,
    ).reshape(2 * rows_here, panel_width)
    product = lax.dot_general(
        factor,
        column_factor,
        (((1,), (1,)), ((), ())),
        precision=lax.Precision.HIGHEST,
        preferred_element_type=jnp.float32,
    )
    return trailing - product


def solution(mesh):
    placed = (P("row", "col"), P("row", "col"), P())
    return jax.shard_map(
        body, mesh=mesh, in_specs=placed, out_specs=P("row", "col"), check_vma=False
    )
```

profile of v0, /device:TPU:1, one launch (start us, length us, event | category | flops | bytes accessed | tf_op | source)
XLA Modules:
  0.0 191.2 jit_solution(5173145244707374873)
XLA Ops:
  6.5 0.0 copy-start
  6.5 0.0 all-reduce.3.cloned.1.call-start
  6.5 32.2 %all_gather.3 = f32[512,256]{0,1:T(8,128)S(1)} all-gather(f32[512,16]{0,1:T(8,128)} %param.4), channel_id=1, replica_groups=mesh['row'=32,'col'=16] {'col'}, dimensions={1}, use_global_device_ids=true | all-gather | bytes 557056 | tf_op jit(solution)/shard_map/all_gather | solution.py:16
  38.7 0.0 copy-done
  38.7 2.0 %broadcast_select_fusion.1 = (f32[512,256]{1,0:T(8,128)}, f32[512,256]{1,0:T(8,128)}, f32[512,256]{1,0:T(8,128)S(1)}) fusion(pred[]{:T(512)S(6)} %eq.6, pred[]{:T(512)S(6)} %eq.7, f32[512,256]{0,1:T(8,128)S(1)} %all_gather.3, f32[256,256]{1,0:T(8,128)S(1)} %copy-done), kind=kOutput, calls=%fused_computation.3 | convolution fusion | flops 402915328 | bytes 2359298 | tf_op jit(solution)/shard_map/dot_general | solution.py:17
  40.7 0.0 copy-start.1
  40.7 0.0 all-reduce.3.cloned.1.call-update
  40.8 139.1 %all-reduce.3.cloned.1.call-done = (f32[2,1,256,256]{3,2,1,0:T(8,128)}, f32[2,1,256,256]{3,2,1,0:T(8,128)}) async-done(((f32[2,1,256,256]{3,2,1,0:T(8,128)}, f32[2,1,256,256]{3,2,1,0:T(8,128)}), (f32[2,1,256,256]{3,2,1,0:T(8,128)}, f32[2,1,256,256]{3,2,1,0:T(8,128)})) %all-reduce.3.cloned.1.call-update) | async-done | bytes 1048592 | tf_op jit(solution)/shard_map/psum | solution.py:9
  179.9 1.3 pad_maximum_fusion
  181.2 0.0 copy-done.1
  181.2 3.2 %convolution_subtract_fusion = f32[512,1024]{1,0:T(8,128)} fusion(f32[512,1024]{1,0:T(8,128)S(1)} %copy-done.1, f32[512,256]{1,0:T(8,128)S(1)} %get-tuple-element.9, f32[1024,256]{1,0:T(8,128)S(1)} %bitcast.11), kind=kOutput, calls=%fused_computation | convolution fusion | flops 1611137024 | bytes 5767168 | tf_op jit(solution)/shard_map/dot_general | solution.py:34
Async XLA Ops:
  6.5 32.2 %copy-start = (f32[256,256]{1,0:T(8,128)S(1)}, f32[256,256]{1,0:T(8,128)}, u32[]{:S(2)}) copy-start(f32[256,256]{1,0:T(8,128)} %param.5) | copy-start | bytes 786436
  6.5 173.4 %all-reduce.3.cloned.1.call-start = ((), (), s32[]{:S(2)}) async-start(), calls=%async_computation | async-start | bytes 2097152 | tf_op jit(solution)/shard_map/psum | solution.py:9
  40.7 140.5 %copy-start.1 = (f32[512,1024]{1,0:T(8,128)S(1)}, f32[512,1024]{1,0:T(8,128)}, u32[]{:S(2)}) copy-start(f32[512,1024]{1,0:T(8,128)} %param.3) | copy-start | bytes 6291460
Sparse Core Ops, SparseCore 0:
  40.9 138.9 all-reduce.2
where the time goes:
time: 191 us
  waiting for transfers between devices  139 us (73%)
  blocking collectives  32.2 us (17%)
  between operations  13.4 us (7%)
  matrix products  5.2 us (3%)
    psum x1, waiting for transfers between devices, from_root(): return lax.psum(block, axis)  139 us
    all_gather x1, blocking collectives, body(): gathered = lax.all_gather(panel, 'col', axis=1, tiled=True)  32.2 us
  transfers between devices with their start and end apart: 1, of which 1 were waited for; matrix products, arithmetic and copies ran while one was open for 0% of the time, Pallas kernels for 0%

commit v1 on v0

v1 whole, which is shorter than its diff:
```python
import functools

import jax
import jax.numpy as jnp
from jax import lax
from jax.experimental import pallas as pl
from jax.experimental.pallas import tpu as pltpu
from jax.sharding import PartitionSpec as P

MESH = pl.DeviceIdType.MESH
LAYERS = 16
SIDE = 4
OFFSETS = {
    8: (0, 0),
    7: (0, 1), 9: (0, 3), 6: (1, 0), 10: (3, 0),
    5: (1, 1), 11: (3, 3), 4: (1, 3), 12: (3, 1), 3: (0, 2), 13: (2, 0),
    2: (1, 2), 14: (3, 2), 1: (2, 1), 15: (2, 3),
    0: (2, 2),
}
HOLDER = [OFFSETS[up][0] * SIDE + OFFSETS[up][1] for up in range(LAYERS)]
CLIMB = [HOLDER.index(place) for place in range(LAYERS)]
OTHERS = sorted(
    [(y, x) for y in range(SIDE) for x in range(SIDE) if (y, x) != (0, 0)],
    key=lambda d: min(d[0], SIDE - d[0]) + min(d[1], SIDE - d[1]),
)
NEAR = (3, -3, 1, -1, 2, -2)


def lookup(table, index):
    value = jnp.int32(table[0])
    for place in range(1, len(table)):
        value = jnp.where(index == place, jnp.int32(table[place]), value)
    return value


def split(x):
    high = x.astype(jnp.bfloat16)
    return high, (x - high.astype(jnp.float32)).astype(jnp.bfloat16)


def gather_kernel(
    slice_ref, lower_ref,
    g_high, g_low, c_high, c_low,
    rows, cols, lower,
    local_sem, row_send, row_recv, hold_sem, cast_send, cast_recv, pass_send, pass_recv,
):
    me, z = lax.axis_index("row"), lax.axis_index("col")
    core, x, y = me % 2, (me // 2) % SIDE, me // (2 * SIDE)
    sibling = (me + 1 - 2 * core, z)

    def above(delta):
        return (me, (z + delta + LAYERS) % LAYERS)

    def beside(dy, dx):
        return ((((y + dy) % SIDE) * SIDE + (x + dx) % SIDE) * 2 + core, z)

    goal = me % LAYERS
    goal_place = lookup(HOLDER, (goal - z + LAYERS) % LAYERS)
    goal_y, goal_x = (y + goal_place // SIDE) % SIDE, (x + goal_place % SIDE) % SIDE
    goal_core = me // LAYERS
    holder = ((goal_y * SIDE + goal_x) * 2 + goal_core, goal)
    owner = z + LAYERS * core
    owner_y, owner_x = owner // (2 * SIDE), (owner // 2) % SIDE

    def place_of(dy, dx):
        return ((y + dy - owner_y + SIDE) % SIDE) * SIDE + (x + dx - owner_x + SIDE) % SIDE

    place = place_of(0, 0)
    giver = (owner, (z - lookup(CLIMB, place) + LAYERS) % LAYERS)

    barrier = pltpu.get_barrier_semaphore()
    partners = [above(d) for d in NEAR] + [beside(*d) for d in OTHERS] + [sibling, giver]
    for partner in partners:
        pl.semaphore_signal(barrier, inc=1, device_id=partner, device_id_type=MESH)
    own = pltpu.make_async_copy(slice_ref, rows.at[z], local_sem.at[0])
    own.start()
    fetch = pltpu.make_async_copy(lower_ref, lower, local_sem.at[1])
    fetch.start()
    own.wait()
    fetch.wait()
    square = lax.dot_general(
        lower[...], lower[...], (((0,), (0,)), ((), ())),
        precision=lax.Precision.HIGHEST, preferred_element_type=jnp.float32,
    )
    lower[...] = square
    pl.semaphore_wait(barrier, len(partners))

    sent, row_sent = [], []

    def send(src, dst, send_sem, recv_sem, device):
        copy = pltpu.make_async_remote_copy(
            src_ref=src, dst_ref=dst, send_sem=send_sem, recv_sem=recv_sem,
            device_id=device, device_id_type=MESH,
        )
        copy.start()
        sent.append(copy)

    def row_slot(offset, part=None):
        ref = rows.at[(z + offset + LAYERS) % LAYERS]
        return ref if part is None else ref.at[pl.ds(8 * part, 8)]

    def row_copy(offset, delta, part=None):
        landed = (offset - delta) % LAYERS
        landed = landed if not part else LAYERS
        slot = row_slot(offset, part)
        send(slot, slot, row_send.at[len(row_sent)], row_recv.at[landed], above(delta))
        row_sent.append(landed)

    def row_wait(offset, part=None):
        slot = row_slot(offset, part)
        semaphore = row_recv.at[LAYERS if part else offset % LAYERS]
        pltpu.make_async_copy(slot, slot, semaphore).wait()

    row_copy(0, 3)
    row_copy(0, -3)
    send(rows.at[z], cols.at[goal_core, goal_place], hold_sem.at[0], hold_sem.at[1], holder)
    row_copy(0, 1)
    row_copy(0, -1)
    for way in (1, -1):
        row_wait(-3 * way)
        row_copy(-3 * way, 3 * way)
        row_copy(-3 * way, way)
        row_copy(-3 * way, -way)

    held = cols.at[core, place]
    pltpu.make_async_copy(held, held, hold_sem.at[1]).wait()
    for i, other in reversed(list(enumerate(OTHERS))):
        send(held, held, cast_send.at[i], cast_recv.at[place], beside(*other))
    send(held, held, pass_send.at[15], pass_recv.at[place], sibling)

    for way in (1, -1):
        row_wait(-6 * way)
        row_copy(-6 * way, 2 * way, 0 if way > 0 else 1)
        row_copy(-6 * way, way)
        row_copy(-6 * way, -way)

    for i, other in enumerate(OTHERS):
        there = place_of(*other)
        slot = cols.at[core, there]
        pltpu.make_async_copy(slot, slot, cast_recv.at[there]).wait()
        send(slot, slot, pass_send.at[i], pass_recv.at[there], sibling)

    def store(source):
        for there in range(LAYERS):
            start = pl.multiple_of(((z - CLIMB[there] + LAYERS) % LAYERS) * 16, 16)
            for k in range(2):
                high, low = split(cols[source, there, :, pl.ds(256 * k, 256)])
                c_high[2 * k + source, pl.ds(start, 16), :] = high
                c_low[2 * k + source, pl.ds(start, 16), :] = low

    store(core)
    for offset in (1, -1, 2, -2, 4, -4, 5, -5, 7, -7):
        row_wait(offset)
    row_wait(8, 0)
    row_wait(8, 1)
    g = lax.dot_general(
        rows[...].reshape(256, 512).T, lower[...], (((1,), (0,)), ((), ())),
        precision=lax.Precision.HIGHEST, preferred_element_type=jnp.float32,
    )
    g_high[...], g_low[...] = split(g)
    for there in range(LAYERS):
        slot = cols.at[1 - core, there]
        pltpu.make_async_copy(slot, slot, pass_recv.at[there]).wait()
    store(1 - core)
    for copy in sent:
        copy.wait_send()


def gather(own_slice, lower_inverse):
    vmem = pl.BlockSpec(memory_space=pltpu.VMEM)
    anywhere = pl.BlockSpec(memory_space=pl.ANY)
    dma = pltpu.SemaphoreType.DMA
    return pl.pallas_call(
        gather_kernel,
        out_shape=[jax.ShapeDtypeStruct((512, 256), jnp.bfloat16)] * 2
        + [jax.ShapeDtypeStruct((4, 256, 256), jnp.bfloat16)] * 2,
        in_specs=[anywhere] * 2,
        out_specs=[vmem] * 4,
        scratch_shapes=[
            pltpu.VMEM((LAYERS, 16, 512), jnp.float32),
            pltpu.VMEM((2, LAYERS, 16, 512), jnp.float32),
            pltpu.VMEM((256, 256), jnp.float32),
            dma((2,)), dma((16,)), dma((LAYERS + 1,)), dma((2,)),
            dma((15,)), dma((LAYERS,)), dma((LAYERS,)), dma((LAYERS,)),
        ],
        compiler_params=pltpu.CompilerParams(
            collective_id=0, has_side_effects=True, vmem_limit_bytes=32 * 2**20
        ),
        name="gather_panel",
    )(own_slice, lower_inverse)


def update_kernel(trailing, g_high, g_low, c_high, c_low, out):
    dot = functools.partial(jnp.dot, preferred_element_type=jnp.float32)
    high = c_high[0]
    product = dot(g_high[...], high) + dot(g_high[...], c_low[0]) + dot(g_low[...], high)
    out[...] = trailing[...] - product


def update(trailing, g_high, g_low, c_high, c_low):
    whole = pl.BlockSpec((512, 256), lambda m: (0, 0))
    block = pl.BlockSpec((1, 256, 256), lambda m: (m, 0, 0))
    tile = pl.BlockSpec((512, 256), lambda m: (0, m))
    return pl.pallas_call(
        update_kernel,
        grid=(4,),
        out_shape=jax.ShapeDtypeStruct((512, 1024), jnp.float32),
        in_specs=[tile, whole, whole, block, block],
        out_specs=tile,
        compiler_params=pltpu.CompilerParams(vmem_limit_bytes=32 * 2**20),
        name="update",
    )(trailing, g_high, g_low, c_high, c_low)


def body(trailing, panel, lower_inverse):
    return update(trailing, *gather(panel.T, lower_inverse))


def solution(mesh):
    placed = (P("row", "col"), P("row", "col"), P())
    return jax.shard_map(
        body, mesh=mesh, in_specs=placed, out_specs=P("row", "col"), check_vma=False
    )
```

time: 191 us -> 43.6 us (0.23)
  waiting for transfers between devices: 139 us -> 0 us
  Pallas kernels: 0 us -> 40.1 us
  blocking collectives: 32.2 us -> 0 us
  between operations: 13.4 us -> 0.02 us
  matrix products: 5.2 us -> 0 us
  local copies, waits for them, and re-layouts: 0.01 us -> 3.29 us
    psum x1 -> x0, waiting for transfers between devices: 139 us -> none  [from_root(): return lax.psum(block, axis)]
    pallas_call x0 -> x2, Pallas kernels: none -> 40.1 us  [the longest x1 37.2 us: gather(): pl.pallas_call(gather_kernel, out_shape=[jax.ShapeDtypeStruct((512, 256),...]
    all_gather x1 -> x0, blocking collectives: 32.2 us -> none  [body(): gathered = lax.all_gather(panel, 'col', axis=1, tiled=True)]
    dot_general x2 -> x0, matrix products: 5.2 us -> none  [the longest x1 3.2 us: body(): lax.dot_general(factor, column_factor, (((1,), (1,)), ((), ())), precisio...]
    unnamed x4 -> x6, local copies, waits for them, and re-layouts: 0.01 us -> 3.29 us
  transfers between devices with their start and end apart: 1 -> 0, of which waited for: 1 -> 0; matrix products, arithmetic and copies ran while one was open for 0% -> 0% of each run, Pallas kernels for 0% -> 0%
where the time goes in v1:
time: 43.6 us; the launch traced here: 43.4 us
  Pallas kernels  40.1 us (92%)
  local copies, waits for them, and re-layouts  3.29 us (8%)
    pallas_call x1, Pallas kernels, gather(): pl.pallas_call(gather_kernel, out_shape=[jax.ShapeDtypeStruct((512, 256),...  37.2 us
    unnamed x6, local copies, waits for them, and re-layouts  3.29 us
    pallas_call x1, Pallas kernels, update(): pl.pallas_call(update_kernel, grid=(4,), out_shape=jax.ShapeDtypeStruct((...  2.86 us

profile of v1, /device:TPU:1, one launch (start us, length us, event | category | flops | bytes accessed | tf_op | source)
XLA Modules:
  0.0 43.4 jit_solution(2009291273279186200)
XLA Ops:
  0.0 0.0 copy-start.1
  0.0 0.9 %copy-done.1 = f32[256,256]{1,0:T(8,128)S(1)} copy-done((f32[256,256]{1,0:T(8,128)S(1)}, f32[256,256]{1,0:T(8,128)}, u32[]{:S(2)}) %copy-start.1) | copy-done | bytes 262168
  1.0 0.0 copy-start.2
  1.0 0.8 %copy-done.2 = f32[512,16]{0,1:T(8,128)S(1)} copy-done((f32[512,16]{0,1:T(8,128)S(1)}, f32[512,16]{0,1:T(8,128)}, u32[]{:S(2)}) %copy-start.2) | copy-done | bytes 32792
  1.7 37.2 %gather_panel.1 = (bf16[512,256]{1,0:T(8,128)(2,1)S(1)}, bf16[512,256]{1,0:T(8,128)(2,1)S(1)}, bf16[4,256,256]{2,1,0:T(8,128)(2,1)S(1)}, bf16[4,256,256]{2,1,0:T(8,128)(2,1)S(1)}) custom-call(f32[16,512]{1,0:T(8,128)S(1)} %bitcast.1, f32[256,256]{1,0:T(8,128)S(1)} %copy-done.1), custom_call_target="tpu_custom_call" | custom-call | tf_op jit(solution)/shard_map/gather_panel/pallas_call | solution.py:173
  38.9 0.0 copy-start
  38.9 1.6 %copy-done = f32[512,1024]{1,0:T(8,128)S(1)} copy-done((f32[512,1024]{1,0:T(8,128)S(1)}, f32[512,1024]{1,0:T(8,128)}, u32[]{:S(2)}) %copy-start) | copy-done | bytes 2097176
  40.5 2.9 %update.1 = f32[512,1024]{1,0:T(8,128)} custom-call(f32[512,1024]{1,0:T(8,128)S(1)} %copy-done, bf16[512,256]{1,0:T(8,128)(2,1)S(1)} %get-tuple-element.9.g_high, bf16[512,256]{1,0:T(8,128)(2,1)S(1)} %get-tuple-element.10.g_low, bf16[4,256,256]{2,1,0:T(8,128)(2,1)S(1)} %get-tuple-element.11.c_high, bf16[4,256,256]{2,1,0:T(8,128)(2,1)S(1)} %get-tuple-element.12.c_low), custom_call_target="tpu_custom_call" | custom-call | tf_op jit(solution)/shard_map/update/pallas_call | solution.py:204
Async XLA Ops:
  0.0 0.9 %copy-start.1 = (f32[256,256]{1,0:T(8,128)S(1)}, f32[256,256]{1,0:T(8,128)}, u32[]{:S(2)}) copy-start(f32[256,256]{1,0:T(8,128)} %lower_ref.1) | copy-start | bytes 786436
  1.0 0.8 %copy-start.2 = (f32[512,16]{0,1:T(8,128)S(1)}, f32[512,16]{0,1:T(8,128)}, u32[]{:S(2)}) copy-start(f32[512,16]{0,1:T(8,128)} %param.4) | copy-start | bytes 98308
  38.9 1.6 %copy-start = (f32[512,1024]{1,0:T(8,128)S(1)}, f32[512,1024]{1,0:T(8,128)}, u32[]{:S(2)}) copy-start(f32[512,1024]{1,0:T(8,128)} %trailing.1) | copy-start | bytes 6291460

commit v2 on v1

--- a/solution.py
+++ b/solution.py
@@ -39,10 +39,10 @@
 
 
 def gather_kernel(
-    slice_ref, lower_ref,
-    g_high, g_low, c_high, c_low,
+    slice_ref, lower_ref, trailing_ref,
+    g_high, g_low, c_high, c_low, near_trailing,
     rows, cols, lower,
-    local_sem, row_send, row_recv, hold_sem, cast_send, cast_recv, pass_send, pass_recv,
+    layer_sem, local_sem, row_send, row_recv, hold_sem, cast_send, cast_recv, pass_send, pass_recv,
 ):
     me, z = lax.axis_index("row"), lax.axis_index("col")
     core, x, y = me % 2, (me // 2) % SIDE, me // (2 * SIDE)
@@ -69,20 +69,18 @@
     giver = (owner, (z - lookup(CLIMB, place) + LAYERS) % LAYERS)
 
     barrier = pltpu.get_barrier_semaphore()
-    partners = [above(d) for d in NEAR] + [beside(*d) for d in OTHERS] + [sibling, giver]
+    across = [beside(0, d) for d in (1, 3, 2)]
+    along = [beside(d, 0) for d in (1, 3, 2)]
+    partners = [giver] + [above(d) for d in NEAR] + across + along + [sibling]
     for partner in partners:
         pl.semaphore_signal(barrier, inc=1, device_id=partner, device_id_type=MESH)
     own = pltpu.make_async_copy(slice_ref, rows.at[z], local_sem.at[0])
     own.start()
     fetch = pltpu.make_async_copy(lower_ref, lower, local_sem.at[1])
     fetch.start()
+    keep = pltpu.make_async_copy(trailing_ref, near_trailing, local_sem.at[2])
+    keep.start()
     own.wait()
-    fetch.wait()
-    square = lax.dot_general(
-        lower[...], lower[...], (((0,), (0,)), ((), ())),
-        precision=lax.Precision.HIGHEST, preferred_element_type=jnp.float32,
-    )
-    lower[...] = square
     pl.semaphore_wait(barrier, len(partners))
 
     sent, row_sent = [], []
@@ -116,12 +114,21 @@
     send(rows.at[z], cols.at[goal_core, goal_place], hold_sem.at[0], hold_sem.at[1], holder)
     row_copy(0, 1)
     row_copy(0, -1)
+    for partner in across:
+        pl.semaphore_signal(layer_sem, inc=1, device_id=partner, device_id_type=MESH)
+    fetch.wait()
+    square = lax.dot_general(
+        lower[...], lower[...], (((0,), (0,)), ((), ())),
+        precision=lax.Precision.HIGHEST, preferred_element_type=jnp.float32,
+    )
+    lower[...] = square
     for way in (1, -1):
         row_wait(-3 * way)
         row_copy(-3 * way, 3 * way)
         row_copy(-3 * way, way)
         row_copy(-3 * way, -way)
 
+    pl.semaphore_wait(layer_sem, len(across))
     held = cols.at[core, place]
     pltpu.make_async_copy(held, held, hold_sem.at[1]).wait()
     for i, other in reversed(list(enumerate(OTHERS))):
@@ -162,58 +169,67 @@
         slot = cols.at[1 - core, there]
         pltpu.make_async_copy(slot, slot, pass_recv.at[there]).wait()
     store(1 - core)
+    keep.wait()
     for copy in sent:
         copy.wait_send()
 
 
-def gather(own_slice, lower_inverse):
+def gather(own_slice, lower_inverse, trailing):
     vmem = pl.BlockSpec(memory_space=pltpu.VMEM)
-    anywhere = pl.BlockSpec(memory_space=pl.ANY)
+    far = pl.BlockSpec(memory_space=pltpu.HBM)
     dma = pltpu.SemaphoreType.DMA
     return pl.pallas_call(
         gather_kernel,
         out_shape=[jax.ShapeDtypeStruct((512, 256), jnp.bfloat16)] * 2
-        + [jax.ShapeDtypeStruct((4, 256, 256), jnp.bfloat16)] * 2,
-        in_specs=[anywhere] * 2,
-        out_specs=[vmem] * 4,
+        + [jax.ShapeDtypeStruct((4, 256, 256), jnp.bfloat16)] * 2
+        + [jax.ShapeDtypeStruct((512, 1024), jnp.float32)],
+        in_specs=[far] * 3,
+        out_specs=[vmem] * 5,
         scratch_shapes=[
             pltpu.VMEM((LAYERS, 16, 512), jnp.float32),
             pltpu.VMEM((2, LAYERS, 16, 512), jnp.float32),
             pltpu.VMEM((256, 256), jnp.float32),
-            dma((2,)), dma((16,)), dma((LAYERS + 1,)), dma((2,)),
+            pltpu.SemaphoreType.REGULAR, dma((3,)), dma((16,)), dma((LAYERS + 1,)), dma((2,)),
             dma((15,)), dma((LAYERS,)), dma((LAYERS,)), dma((LAYERS,)),
         ],
         compiler_params=pltpu.CompilerParams(
             collective_id=0, has_side_effects=True, vmem_limit_bytes=32 * 2**20
         ),
         name="gather_panel",
-    )(own_slice, lower_inverse)
-
-
-def update_kernel(trailing, g_high, g_low, c_high, c_low, out):
+    )(*[pltpu.with_memory_space_constraint(a, pltpu.HBM) for a in (own_slice, lower_inverse, trailing)])
+
+
+def update_kernel(g_high, g_low, c_high, c_low, trailing, out, done, sem):
     dot = functools.partial(jnp.dot, preferred_element_type=jnp.float32)
-    high = c_high[0]
-    product = dot(g_high[...], high) + dot(g_high[...], c_low[0]) + dot(g_low[...], high)
-    out[...] = trailing[...] - product
-
-
-def update(trailing, g_high, g_low, c_high, c_low):
-    whole = pl.BlockSpec((512, 256), lambda m: (0, 0))
-    block = pl.BlockSpec((1, 256, 256), lambda m: (m, 0, 0))
-    tile = pl.BlockSpec((512, 256), lambda m: (0, m))
+    copies = []
+    for m in range(4):
+        block = (slice(None), pl.ds(256 * m, 256))
+        product = dot(g_high[...], c_high[m]) + dot(g_high[...], c_low[m]) + dot(g_low[...], c_high[m])
+        done[block] = trailing[block] - product
+        copies.append(pltpu.make_async_copy(done.at[block], out.at[block], sem.at[m]))
+        copies[-1].start()
+    for copy in copies:
+        copy.wait()
+
+
+def update(*operands):
+    vmem = pl.BlockSpec(memory_space=pltpu.VMEM)
     return pl.pallas_call(
         update_kernel,
-        grid=(4,),
         out_shape=jax.ShapeDtypeStruct((512, 1024), jnp.float32),
-        in_specs=[tile, whole, whole, block, block],
-        out_specs=tile,
+        in_specs=[vmem] * 5,
+        out_specs=pl.BlockSpec(memory_space=pltpu.HBM),
+        scratch_shapes=[
+            pltpu.VMEM((512, 1024), jnp.float32),
+            pltpu.SemaphoreType.DMA((4,)),
+        ],
         compiler_params=pltpu.CompilerParams(vmem_limit_bytes=32 * 2**20),
         name="update",
-    )(trailing, g_high, g_low, c_high, c_low)
+    )(*operands)
 
 
 def body(trailing, panel, lower_inverse):
-    return update(trailing, *gather(panel.T, lower_inverse))
+    return update(*gather(panel.T, lower_inverse, trailing))
 
 
 def solution(mesh):

time: 43.6 us -> 35.7 us (0.82)
  Pallas kernels: 40.1 us -> 35.6 us
  local copies, waits for them, and re-layouts: 3.29 us -> 0 us
    pallas_call x1, Pallas kernels: 37.2 us -> 33.5 us  [gather(): pl.pallas_call(gather_kernel, out_shape=[jax.ShapeDtypeStruct((512, 256),...]
    unnamed x6 -> x0, local copies, waits for them, and re-layouts: 3.29 us -> none
    pallas_call x1, Pallas kernels: 2.86 us -> 2.07 us  [update(): pl.pallas_call(update_kernel, out_shape=jax.ShapeDtypeStruct((512, 1024),...]
where the time goes in v2:
time: 35.7 us; the launch traced here: 35.6 us
  Pallas kernels  35.6 us (100%)
    pallas_call x1, Pallas kernels, gather(): pl.pallas_call(gather_kernel, out_shape=[jax.ShapeDtypeStruct((512, 256),...  33.5 us
    pallas_call x1, Pallas kernels, update(): pl.pallas_call(update_kernel, out_shape=jax.ShapeDtypeStruct((512, 1024),...  2.07 us

profile of v2, /device:TPU:1, one launch (start us, length us, event | category | flops | bytes accessed | tf_op | source)
XLA Modules:
  0.0 35.6 jit_solution(13083535602617514032)
XLA Ops:
  0.0 33.5 %gather_panel.1 = (bf16[512,256]{1,0:T(8,128)(2,1)S(1)}, bf16[512,256]{1,0:T(8,128)(2,1)S(1)}, bf16[4,256,256]{2,1,0:T(8,128)(2,1)S(1)}, bf16[4,256,256]{2,1,0:T(8,128)(2,1)S(1)}, f32[512,1024]{1,0:T(8,128)S(1)}) custom-call(f32[16,512]{1,0:T(8,128)} %bitcast.1, f32[256,256]{1,0:T(8,128)} %lower_ref.1, f32[512,1024]{1,0:T(8,128)} %trailing_ref.1), custom_call_target="tpu_custom_call" | custom-call | tf_op jit(solution)/shard_map/gather_panel/pallas_call | solution.py:181
  33.5 2.1 %update.1 = f32[512,1024]{1,0:T(8,128)} custom-call(bf16[512,256]{1,0:T(8,128)(2,1)S(1)} %get-tuple-element.10.g_high, bf16[512,256]{1,0:T(8,128)(2,1)S(1)} %get-tuple-element.11.g_low, bf16[4,256,256]{2,1,0:T(8,128)(2,1)S(1)} %get-tuple-element.12.c_high, bf16[4,256,256]{2,1,0:T(8,128)(2,1)S(1)} %get-tuple-element.13.c_low, ...), custom_call_target="tpu_custom_call" | custom-call | tf_op jit(solution)/shard_map/update/pallas_call | solution.py:217

commit v3 on v2

v3 whole, which is shorter than its diff:
```python
import functools

import jax
import jax.numpy as jnp
from jax import lax
from jax.experimental import pallas as pl
from jax.experimental.pallas import tpu as pltpu
from jax.sharding import PartitionSpec as P

MESH = pl.DeviceIdType.MESH
LAYERS = 16
SIDE = 4
FAR = {8: (0, 0), 7: (0, 1), 9: (0, 3), 6: (1, 0), 10: (0, 2), 5: (1, 1), 11: (1, 3), 4: (1, 2)}
CLOSE = {12: (0, 0), 3: (0, 1), 13: (0, 3), 2: (1, 0), 14: (0, 2), 1: (1, 1), 15: (1, 3), 0: (1, 2)}
HOLDER = [SIDE * y + x for _, (y, x) in sorted({**FAR, **CLOSE}.items())]
CLIMB = [sorted(held, key=lambda up: HOLDER[up]) for held in (CLOSE, FAR)]
PASSED = [(0, 15, 14, 13, 12, 1, 2, 3), (11, 4, 10, 5, 9, 6, 7, 8)]
FIRST = 12
OTHERS = sorted(
    [(y, x) for y in range(SIDE) for x in range(SIDE) if (y, x) != (0, 0)],
    key=lambda d: min(d[0], SIDE - d[0]) + min(d[1], SIDE - d[1]),
)
RELAYED = {3: 0, -3: 1, 6: 2, -6: 3}
NEAR = (3, -3, 1, -1, 2, -2)


def lookup(table, index):
    value = jnp.int32(table[0])
    for place in range(1, len(table)):
        value = jnp.where(index == place, jnp.int32(table[place]), value)
    return value


def split(x):
    high = x.astype(jnp.bfloat16)
    return high, (x - high.astype(jnp.float32)).astype(jnp.bfloat16)


def product(g_high, g_low, c_high, c_low, k):
    dot = functools.partial(jnp.dot, preferred_element_type=jnp.float32)
    high = c_high[k]
    return dot(g_high[...], high) + dot(g_high[...], c_low[k]) + dot(g_low[...], high)


def gather_kernel(
    slice_ref, lower_ref, trailing_ref,
    g_high, g_low, c_high, c_low, near_trailing,
    rows, cols, lower, relay,
    layer_sem, local_sem, row_send, row_recv, relay_recv, hold_sem, cast_send, cast_recv, pass_send, pass_recv,
):
    me, z = lax.axis_index("row"), lax.axis_index("col")
    core, x, y = me % 2, (me // 2) % SIDE, me // (2 * SIDE)
    sibling = (me + 1 - 2 * core, z)

    def above(delta):
        return (me, (z + delta + LAYERS) % LAYERS)

    def beside(dy, dx):
        return ((((y + dy) % SIDE) * SIDE + (x + dx) % SIDE) * 2 + core, z)

    barrier = pltpu.get_barrier_semaphore()
    across = [beside(0, d) for d in (1, 3, 2)]
    along = [beside(d, 0) for d in (1, 3, 2)]
    for partner in across + along + [sibling]:
        pl.semaphore_signal(barrier, inc=1, device_id=partner, device_id_type=MESH)

    def greet(steps, to_core):
        for delta in steps:
            partner = (me - core + to_core, (z + delta + LAYERS) % LAYERS)
            pl.semaphore_signal(barrier, inc=1, device_id=partner, device_id_type=MESH)

    @pl.when(core == 0)
    def _():
        greet((2, -2, 1, -1), 1)
        greet((1, -1), 0)

    @pl.when(core == 1)
    def _():
        greet((3, -3, 2, -2, 1, -1), 1)
        greet((3, -3), 0)

    goal = me % LAYERS
    climb = (goal - z + LAYERS) % LAYERS
    spot = lookup(HOLDER, climb)
    goal_core = jnp.where((climb >= 4) & (climb < 12), 1, 0)
    goal_place = spot + 2 * SIDE * (me // LAYERS)
    goal_y, goal_x = (y + spot // SIDE) % SIDE, (x + spot % SIDE) % SIDE
    holder = ((goal_y * SIDE + goal_x) * 2 + goal_core, goal)
    owner_y, owner_x = z // (2 * SIDE), (z // 2) % SIDE

    def place_of(dy, dx):
        return ((y + dy - owner_y + SIDE) % SIDE) * SIDE + (x + dx - owner_x + SIDE) % SIDE

    place = place_of(0, 0)
    risen = jnp.where(core == 1, lookup(CLIMB[1], place % 8), lookup(CLIMB[0], place % 8))
    giver = (z + LAYERS * (place // 8), (z - risen + LAYERS) % LAYERS)

    pl.semaphore_signal(barrier, inc=1, device_id=giver, device_id_type=MESH)
    own = pltpu.make_async_copy(slice_ref, rows.at[z], local_sem.at[0])
    own.start()
    fetch = pltpu.make_async_copy(lower_ref, lower, local_sem.at[1])
    fetch.start()
    for m in range(4):
        pltpu.make_async_copy(
            trailing_ref.at[:, pl.ds(256 * m, 256)], near_trailing.at[m], local_sem.at[2]
        ).start()
    own.wait()
    pl.semaphore_wait(barrier, jnp.where(core == 0, 12, 18))

    def send(src, dst, send_sem, recv_sem, device):
        pltpu.make_async_remote_copy(
            src_ref=src, dst_ref=dst, send_sem=send_sem, recv_sem=recv_sem,
            device_id=device, device_id_type=MESH,
        ).start()

    def wait(ref, semaphore):
        pltpu.make_async_copy(ref, ref, semaphore).wait()

    def row_slot(offset, part=None):
        ref = rows.at[(z + offset + LAYERS) % LAYERS]
        return ref if part is None else ref.at[pl.ds(8 * part, 8)]

    def row_copy(offset, delta, part=None):
        slot = row_slot(offset, part)
        send(slot, slot, row_send.at[0], row_recv.at[RELAYED.get(offset - delta, 4)], above(delta))

    def guest_copy(offset, delta, part=None):
        half = pl.ds(0, 16) if part is None else pl.ds(8 * part, 8)
        slot = relay.at[RELAYED[offset], half]
        if delta and offset - delta in RELAYED:
            index = RELAYED[offset - delta]
            send(slot, relay.at[index], row_send.at[1], relay_recv.at[index], above(delta))
        else:
            there = (me - 1, (z + delta + LAYERS) % LAYERS)
            send(slot, rows.at[(z + offset + LAYERS) % LAYERS, half], row_send.at[1], row_recv.at[4], there)

    def row_wait(offset):
        wait(row_slot(offset), row_recv.at[RELAYED[offset]])

    send(rows.at[z], cols.at[goal_core, goal_place], hold_sem.at[0], hold_sem.at[1], holder)

    @pl.when(core == 0)
    def _():
        for delta in (3, -3):
            index = RELAYED[-delta]
            there = (me + 1, (z + delta + LAYERS) % LAYERS)
            send(rows.at[z], relay.at[index], row_send.at[0], relay_recv.at[index], there)

    @pl.when(core == 1)
    def _():
        row_copy(0, 3)
        row_copy(0, -3)

    for partner in across:
        pl.semaphore_signal(layer_sem, inc=1, device_id=partner, device_id_type=MESH)
    fetch.wait()
    square = lax.dot_general(
        lower[...], lower[...], (((0,), (0,)), ((), ())),
        precision=lax.Precision.HIGHEST, preferred_element_type=jnp.float32,
    )
    lower[...] = square
    @pl.when(core == 1)
    def _():
        for way in (1, -1):
            row_wait(-3 * way)
            row_copy(-3 * way, 3 * way)
            row_copy(-3 * way, way)
            row_copy(-3 * way, -way)
        for way in (1, -1):
            wait(relay.at[RELAYED[-3 * way]], relay_recv.at[RELAYED[-3 * way]])
            for delta in (3 * way, way, -way, 0):
                guest_copy(-3 * way, delta)

    pl.semaphore_wait(layer_sem, len(across))
    held = cols.at[core, place]
    wait(held, hold_sem.at[1])
    for other in OTHERS[::-1]:
        send(held, held, cast_send, cast_recv.at[place], beside(*other))
    late = [HOLDER[up] for up in PASSED[0][FIRST // 2 :]], [HOLDER[up] for up in PASSED[1][FIRST // 2 :]]
    turn = [sum(jnp.where(place % 8 == there, 1, 0) for there in late[c]) for c in (0, 1)]
    send(held, held, pass_send, pass_recv.at[jnp.where(core == 1, turn[1], turn[0])], sibling)
    row_copy(0, 1)
    row_copy(0, -1)

    @pl.when(core == 1)
    def _():
        for way in (1, -1):
            row_wait(-6 * way)
            row_copy(-6 * way, 2 * way, 0 if way > 0 else 1)
            row_copy(-6 * way, way)
            row_copy(-6 * way, -way)
        for way in (1, -1):
            wait(relay.at[RELAYED[-6 * way]], relay_recv.at[RELAYED[-6 * way]])
            guest_copy(-6 * way, 2 * way, 0 if way > 0 else 1)
            for delta in (way, -way, 0):
                guest_copy(-6 * way, delta)

    def slot_of(holding, i):
        up = [PASSED[c][i // 2] for c in (0, 1)]
        there = [HOLDER[up[c]] + 8 * (i % 2) for c in (0, 1)]
        return jnp.where(holding == 1, there[1], there[0]), jnp.where(holding == 1, up[1], up[0])

    def store(holding, i):
        there, up = slot_of(holding, i)
        start = pl.multiple_of(((z - up + LAYERS) % LAYERS) * 16, 16)
        for k in range(2):
            high, low = split(cols[holding, there, :, pl.ds(256 * k, 256)])
            c_high[2 * k + i % 2, pl.ds(start, 16), :] = high
            c_low[2 * k + i % 2, pl.ds(start, 16), :] = low

    for i in range(LAYERS):
        there, _ = slot_of(core, i)
        slot = cols.at[core, there]

        @pl.when(there != place)
        def _():
            wait(slot, cast_recv.at[there])
            send(slot, slot, pass_send, pass_recv.at[i // FIRST], sibling)

        store(core, i)

    pl.when(core == 0)(lambda: wait(rows.at[pl.ds(0, 15)], row_recv.at[4]))
    pl.when(core == 1)(lambda: wait(rows.at[pl.ds(0, 11)], row_recv.at[4]))
    g = lax.dot_general(
        rows[...].reshape(256, 512).T, lower[...], (((1,), (0,)), ((), ())),
        precision=lax.Precision.HIGHEST, preferred_element_type=jnp.float32,
    )
    g_high[...], g_low[...] = split(g)
    wait(near_trailing, local_sem.at[2])

    @pl.when(core == 0)
    def _():
        wait(rows.at[pl.ds(0, 4)], row_send.at[0])

    @pl.when(core == 1)
    def _():
        wait(rows.at[pl.ds(0, 15)], row_send.at[0])
        wait(rows.at[pl.ds(0, 15)], row_send.at[1])

    wait(rows.at[z], hold_sem.at[0])
    wait(cols.at[core, pl.ds(0, 15)], cast_send)
    wait(cols.at[core], pass_send)
    for i in range(LAYERS):
        if i == 0:
            wait(cols.at[1 - core, pl.ds(0, FIRST)], pass_recv.at[0])
        if i == FIRST:
            wait(cols.at[1 - core, pl.ds(0, LAYERS - FIRST)], pass_recv.at[1])
        store(1 - core, i)


def gather(own_slice, lower_inverse, trailing):
    vmem = pl.BlockSpec(memory_space=pltpu.VMEM)
    far = pl.BlockSpec(memory_space=pltpu.HBM)
    dma = pltpu.SemaphoreType.DMA
    return pl.pallas_call(
        gather_kernel,
        out_shape=[jax.ShapeDtypeStruct((512, 256), jnp.bfloat16)] * 2
        + [jax.ShapeDtypeStruct((4, 256, 256), jnp.bfloat16)] * 2
        + [jax.ShapeDtypeStruct((4, 512, 256), jnp.float32)],
        in_specs=[far] * 3,
        out_specs=[vmem] * 5,
        scratch_shapes=[
            pltpu.VMEM((LAYERS, 16, 512), jnp.float32),
            pltpu.VMEM((2, LAYERS, 16, 512), jnp.float32),
            pltpu.VMEM((256, 256), jnp.float32),
            pltpu.VMEM((4, 16, 512), jnp.float32),
            pltpu.SemaphoreType.REGULAR, dma((3,)), dma((2,)), dma((5,)), dma((4,)), dma((2,)),
            dma, dma((LAYERS,)), dma, dma((2,)),
        ],
        compiler_params=pltpu.CompilerParams(
            collective_id=0, has_side_effects=True, vmem_limit_bytes=32 * 2**20
        ),
        name="gather_panel",
    )(*[pltpu.with_memory_space_constraint(a, pltpu.HBM) for a in (own_slice, lower_inverse, trailing)])


def update_kernel(g_high, g_low, c_high, c_low, trailing, out, done, sem):
    copies = []
    for m in range(4):
        done[m] = trailing[m] - product(g_high, g_low, c_high, c_low, m)
        copies.append(pltpu.make_async_copy(done.at[m], out.at[:, pl.ds(256 * m, 256)], sem.at[m]))
        copies[-1].start()
    for copy in copies:
        copy.wait()


def update(*operands):
    vmem = pl.BlockSpec(memory_space=pltpu.VMEM)
    return pl.pallas_call(
        update_kernel,
        out_shape=jax.ShapeDtypeStruct((512, 1024), jnp.float32),
        in_specs=[vmem] * 5,
        out_specs=pl.BlockSpec(memory_space=pltpu.HBM),
        scratch_shapes=[
            pltpu.VMEM((4, 512, 256), jnp.float32),
            pltpu.SemaphoreType.DMA((4,)),
        ],
        compiler_params=pltpu.CompilerParams(vmem_limit_bytes=32 * 2**20),
        name="update",
    )(*operands)


def body(trailing, panel, lower_inverse):
    return update(*gather(panel.T, lower_inverse, trailing))


def solution(mesh):
    placed = (P("row", "col"), P("row", "col"), P())
    return jax.shard_map(
        body, mesh=mesh, in_specs=placed, out_specs=P("row", "col"), check_vma=False
    )
```

time: 35.7 us -> 33.5 us (0.938)
  Pallas kernels: 35.6 us -> 33.4 us
    pallas_call x1, Pallas kernels: 33.5 us -> 31.3 us  [gather(): pl.pallas_call(gather_kernel, out_shape=[jax.ShapeDtypeStruct((512, 256),...]
where the time goes in v3:
time: 33.5 us; the launch traced here: 33.4 us
  Pallas kernels  33.4 us (100%)
    pallas_call x1, Pallas kernels, gather(): pl.pallas_call(gather_kernel, out_shape=[jax.ShapeDtypeStruct((512, 256),...  31.3 us
    pallas_call x1, Pallas kernels, update(): pl.pallas_call(update_kernel, out_shape=jax.ShapeDtypeStruct((512, 1024),...  2.06 us

profile of v3, /device:TPU:1, one launch (start us, length us, event | category | flops | bytes accessed | tf_op | source)
XLA Modules:
  0.0 33.4 jit_solution(1129543556791616401)
XLA Ops:
  0.0 31.3 %gather_panel.1 = (bf16[512,256]{1,0:T(8,128)(2,1)S(1)}, bf16[512,256]{1,0:T(8,128)(2,1)S(1)}, bf16[4,256,256]{2,1,0:T(8,128)(2,1)S(1)}, bf16[4,256,256]{2,1,0:T(8,128)(2,1)S(1)}, f32[4,512,256]{2,1,0:T(8,128)S(1)}) custom-call(f32[16,512]{1,0:T(8,128)} %bitcast.1, f32[256,256]{1,0:T(8,128)} %lower_ref.1, f32[512,1024]{1,0:T(8,128)} %trailing_ref.1), custom_call_target="tpu_custom_call" | custom-call | tf_op jit(solution)/shard_map/gather_panel/pallas_call | solution.py:255
  31.3 2.1 %update.1 = f32[512,1024]{1,0:T(8,128)} custom-call(bf16[512,256]{1,0:T(8,128)(2,1)S(1)} %get-tuple-element.10.g_high, bf16[512,256]{1,0:T(8,128)(2,1)S(1)} %get-tuple-element.11.g_low, bf16[4,256,256]{2,1,0:T(8,128)(2,1)S(1)} %get-tuple-element.12.c_high, bf16[4,256,256]{2,1,0:T(8,128)(2,1)S(1)} %get-tuple-element.13.c_low, ...), custom_call_target="tpu_custom_call" | custom-call | tf_op jit(solution)/shard_map/update/pallas_call | solution.py:289

commit v4 on v3

v4 whole, which is shorter than its diff:
```python
import functools

import jax
import jax.numpy as jnp
from jax import lax
from jax.experimental import pallas as pl
from jax.experimental.pallas import tpu as pltpu
from jax.sharding import PartitionSpec as P

MESH = pl.DeviceIdType.MESH
LAYERS = 16
SIDE = 4
FAR = {8: (0, 0), 7: (0, 1), 9: (0, 3), 6: (1, 0), 10: (0, 2), 5: (1, 1), 11: (1, 3), 4: (1, 2)}
CLOSE = {12: (0, 0), 3: (0, 1), 13: (0, 3), 2: (1, 0), 14: (0, 2), 1: (1, 1), 15: (1, 3), 0: (1, 2)}
HOLDER = [SIDE * y + x for _, (y, x) in sorted({**FAR, **CLOSE}.items())]
CLIMB = [sorted(held, key=lambda up: HOLDER[up]) for held in (CLOSE, FAR)]
BATCH = 4
BATCHES = (1, 3, 0, 2)
OTHERS = sorted(
    [(y, x) for y in range(SIDE) for x in range(SIDE) if (y, x) != (0, 0)],
    key=lambda d: min(d[0], SIDE - d[0]) + min(d[1], SIDE - d[1]),
)
RELAYED = {3: 0, -3: 1, 6: 2, -6: 3}
NEAR = (3, -3, 1, -1, 2, -2)


def lookup(table, index):
    value = jnp.int32(table[0])
    for place in range(1, len(table)):
        value = jnp.where(index == place, jnp.int32(table[place]), value)
    return value


def split(x):
    high = x.astype(jnp.bfloat16)
    return high, (x - high.astype(jnp.float32)).astype(jnp.bfloat16)


def gather_kernel(
    slice_ref, lower_ref, trailing_ref,
    g_high, g_low, c_high, c_low, near_trailing,
    rows, cols, lower, relay,
    near_sem, layer_sem, local_sem, row_send, row_recv, relay_recv, hold_sem, cast_send, cast_recv, pass_send, pass_recv,
):
    me, z = lax.axis_index("row"), lax.axis_index("col")
    core, x, y = me % 2, (me // 2) % SIDE, me // (2 * SIDE)
    sibling = (me + 1 - 2 * core, z)

    def above(delta):
        return (me, (z + delta + LAYERS) % LAYERS)

    def beside(dy, dx):
        return ((((y + dy) % SIDE) * SIDE + (x + dx) % SIDE) * 2 + core, z)

    barrier = pltpu.get_barrier_semaphore()
    across = [beside(0, d) for d in (1, 3, 2)]
    along = [beside(d, 0) for d in (1, 3, 2)]
    def tell(semaphore, partner):
        pl.semaphore_signal(semaphore, inc=1, device_id=partner, device_id_type=MESH)

    tell(barrier, sibling)

    @pl.when(core == 1)
    def _():
        for delta in (3, -3):
            tell(barrier, (me - 1, above(delta)[1]))
        for partner in [above(delta) for delta in NEAR] + across + along:
            tell(barrier, partner)

    goal = me % LAYERS
    climb = (goal - z + LAYERS) % LAYERS
    spot = lookup(HOLDER, climb)
    goal_core = jnp.where((climb >= 4) & (climb < 12), 1, 0)
    goal_place = spot + 2 * SIDE * (me // LAYERS)
    goal_y, goal_x = (y + spot // SIDE) % SIDE, (x + spot % SIDE) % SIDE
    holder = ((goal_y * SIDE + goal_x) * 2 + goal_core, goal)
    owner_y, owner_x = z // (2 * SIDE), (z // 2) % SIDE

    def place_of(dy, dx):
        return ((y + dy - owner_y + SIDE) % SIDE) * SIDE + (x + dx - owner_x + SIDE) % SIDE

    place = place_of(0, 0)
    risen = jnp.where(core == 1, lookup(CLIMB[1], place % 8), lookup(CLIMB[0], place % 8))
    giver = (z + LAYERS * (place // 8), (z - risen + LAYERS) % LAYERS)

    tell(barrier, giver)
    own = pltpu.make_async_copy(slice_ref, rows.at[z], local_sem.at[0])
    own.start()
    fetch = pltpu.make_async_copy(lower_ref, lower, local_sem.at[1])
    fetch.start()
    keep = pltpu.make_async_copy(trailing_ref, near_trailing, local_sem.at[2])
    keep.start()
    own.wait()
    pl.semaphore_wait(barrier, jnp.where(core == 0, 4, 14))

    def send(src, dst, send_sem, recv_sem, device):
        pltpu.make_async_remote_copy(
            src_ref=src, dst_ref=dst, send_sem=send_sem, recv_sem=recv_sem,
            device_id=device, device_id_type=MESH,
        ).start()

    def wait(ref, semaphore):
        pltpu.make_async_copy(ref, ref, semaphore).wait()

    def row_slot(offset, part=None):
        ref = rows.at[(z + offset + LAYERS) % LAYERS]
        return ref if part is None else ref.at[pl.ds(8 * part, 8)]

    def row_copy(offset, delta, part=None):
        slot = row_slot(offset, part)
        send(slot, slot, row_send.at[0], row_recv.at[RELAYED.get(offset - delta, 4)], above(delta))

    def guest_copy(offset, delta, part=None):
        half = pl.ds(0, 16) if part is None else pl.ds(8 * part, 8)
        slot = relay.at[RELAYED[offset], half]
        if delta and offset - delta in RELAYED:
            index = RELAYED[offset - delta]
            send(slot, relay.at[index], row_send.at[1], relay_recv.at[index], above(delta))
        else:
            there = (me - 1, (z + delta + LAYERS) % LAYERS)
            send(slot, rows.at[(z + offset + LAYERS) % LAYERS, half], row_send.at[1], row_recv.at[4], there)

    def row_wait(offset):
        wait(row_slot(offset), row_recv.at[RELAYED[offset]])

    def to_holder():
        send(rows.at[z], cols.at[goal_core, goal_place], hold_sem.at[0], hold_sem.at[1], holder)

    pl.when(core == 0)(to_holder)

    @pl.when(core == 0)
    def _():
        for delta in (3, -3):
            index = RELAYED[-delta]
            there = (me + 1, (z + delta + LAYERS) % LAYERS)
            send(rows.at[z], relay.at[index], row_send.at[0], relay_recv.at[index], there)

    @pl.when(core == 1)
    def _():
        row_copy(0, 3)
        row_copy(0, -3)
        to_holder()

    @pl.when(core == 1)
    def _():
        for partner in along + [above(delta) for delta in (1, -1, 2, -2)]:
            tell(near_sem, partner)

    fetch.wait()
    square = lax.dot_general(
        lower[...], lower[...], (((0,), (0,)), ((), ())),
        precision=lax.Precision.HIGHEST, preferred_element_type=jnp.float32,
    )
    lower[...] = square

    @pl.when(core == 1)
    def _():
        pl.semaphore_wait(near_sem, 7)
        for partner in across:
            tell(layer_sem, partner)
        pl.semaphore_wait(layer_sem, 3)
        tell(layer_sem, sibling)

    @pl.when(core == 1)
    def _():
        for way in (1, -1):
            row_wait(-3 * way)
            row_copy(-3 * way, 3 * way)
            row_copy(-3 * way, way)
            row_copy(-3 * way, -way)
        for way in (1, -1):
            wait(relay.at[RELAYED[-3 * way]], relay_recv.at[RELAYED[-3 * way]])
            for delta in (3 * way, way, -way, 0):
                guest_copy(-3 * way, delta)

    pl.when(core == 0)(lambda: pl.semaphore_wait(layer_sem, 1))
    held = cols.at[core, place]
    wait(held, hold_sem.at[1])
    for other in OTHERS[::-1]:
        send(held, held, cast_send, cast_recv.at[place // BATCH], beside(*other))
    row_copy(0, 1)
    row_copy(0, -1)

    @pl.when(core == 1)
    def _():
        for way in (1, -1):
            row_wait(-6 * way)
            row_copy(-6 * way, 2 * way, 0 if way > 0 else 1)
            row_copy(-6 * way, way)
            row_copy(-6 * way, -way)
        for way in (1, -1):
            wait(relay.at[RELAYED[-6 * way]], relay_recv.at[RELAYED[-6 * way]])
            guest_copy(-6 * way, 2 * way, 0 if way > 0 else 1)
            for delta in (way, -way, 0):
                guest_copy(-6 * way, delta)

    def store(holding, batch):
        for there in range(BATCH * batch, BATCH * (batch + 1)):
            risen = jnp.where(holding == 1, CLIMB[1][there % 8], CLIMB[0][there % 8])
            start = pl.multiple_of(((z - risen + LAYERS) % LAYERS) * 16, 16)
            for k in range(2):
                columns = pl.ds(256 * (2 * k + there // 8), 256)
                high, low = split(cols[holding, there, :, pl.ds(256 * k, 256)])
                c_high[pl.ds(start, 16), columns] = high
                c_low[pl.ds(start, 16), columns] = low

    def take(batch):
        slots = cols.at[core, pl.ds(BATCH * batch, BATCH)]
        held_here = place // BATCH == batch
        pl.when(held_here)(lambda: wait(cols.at[core, pl.ds(0, BATCH - 1)], cast_recv.at[batch]))
        pl.when(jnp.logical_not(held_here))(lambda: wait(slots, cast_recv.at[batch]))
        send(slots, slots, pass_send, pass_recv.at[batch], sibling)
        store(core, batch)

    def transform(slices):
        wait(rows.at[pl.ds(0, slices)], row_recv.at[4])
        g = lax.dot_general(
            rows[...].reshape(256, 512).T, lower[...], (((1,), (0,)), ((), ())),
            precision=lax.Precision.HIGHEST, preferred_element_type=jnp.float32,
        )
        g_high[...], g_low[...] = split(g)

    for batch in BATCHES:
        take(batch)
    pl.when(core == 1)(lambda: transform(11))
    pl.when(core == 0)(lambda: transform(15))
    keep.wait()

    @pl.when(core == 0)
    def _():
        wait(rows.at[pl.ds(0, 4)], row_send.at[0])

    @pl.when(core == 1)
    def _():
        wait(rows.at[pl.ds(0, 15)], row_send.at[0])
        wait(rows.at[pl.ds(0, 15)], row_send.at[1])

    wait(rows.at[z], hold_sem.at[0])
    wait(cols.at[core, pl.ds(0, 15)], cast_send)
    wait(cols.at[core], pass_send)
    for batch in BATCHES:
        wait(cols.at[1 - core, pl.ds(BATCH * batch, BATCH)], pass_recv.at[batch])
        store(1 - core, batch)


def gather(own_slice, lower_inverse, trailing):
    vmem = pl.BlockSpec(memory_space=pltpu.VMEM)
    far = pl.BlockSpec(memory_space=pltpu.HBM)
    dma = pltpu.SemaphoreType.DMA
    return pl.pallas_call(
        gather_kernel,
        out_shape=[jax.ShapeDtypeStruct((512, 256), jnp.bfloat16)] * 2
        + [jax.ShapeDtypeStruct((256, 1024), jnp.bfloat16)] * 2
        + [jax.ShapeDtypeStruct((512, 1024), jnp.float32)],
        in_specs=[far] * 3,
        out_specs=[vmem] * 5,
        scratch_shapes=[
            pltpu.VMEM((LAYERS, 16, 512), jnp.float32),
            pltpu.VMEM((2, LAYERS, 16, 512), jnp.float32),
            pltpu.VMEM((256, 256), jnp.float32),
            pltpu.VMEM((4, 16, 512), jnp.float32),
            pltpu.SemaphoreType.REGULAR, pltpu.SemaphoreType.REGULAR, dma((3,)), dma((2,)), dma((5,)), dma((4,)), dma((2,)),
            dma, dma((4,)), dma, dma((4,)),
        ],
        compiler_params=pltpu.CompilerParams(
            collective_id=0, has_side_effects=True, vmem_limit_bytes=32 * 2**20
        ),
        name="gather_panel",
    )(*[pltpu.with_memory_space_constraint(a, pltpu.HBM) for a in (own_slice, lower_inverse, trailing)])


def update_kernel(g_high, g_low, c_high, c_low, trailing, out, done, sem):
    dot = functools.partial(jnp.dot, preferred_element_type=jnp.float32)
    copies = []
    for part in range(4):
        r = pl.ds(128 * part, 128)
        product = dot(g_high[r], c_high[...]) + dot(g_high[r], c_low[...]) + dot(g_low[r], c_high[...])
        done[r] = trailing[r] - product
        copies.append(pltpu.make_async_copy(done.at[r], out.at[r], sem.at[part]))
        copies[-1].start()
    for copy in copies:
        copy.wait()


def update(*operands):
    vmem = pl.BlockSpec(memory_space=pltpu.VMEM)
    return pl.pallas_call(
        update_kernel,
        out_shape=jax.ShapeDtypeStruct((512, 1024), jnp.float32),
        in_specs=[vmem] * 5,
        out_specs=pl.BlockSpec(memory_space=pltpu.HBM),
        scratch_shapes=[
            pltpu.VMEM((512, 1024), jnp.float32),
            pltpu.SemaphoreType.DMA((4,)),
        ],
        compiler_params=pltpu.CompilerParams(vmem_limit_bytes=32 * 2**20),
        name="update",
    )(*operands)


def body(trailing, panel, lower_inverse):
    return update(*gather(panel.T, lower_inverse, trailing))


def solution(mesh):
    placed = (P("row", "col"), P("row", "col"), P())
    return jax.shard_map(
        body, mesh=mesh, in_specs=placed, out_specs=P("row", "col"), check_vma=False
    )
```

time: 33.5 us -> 33.2 us (level)
  no operation moved by 1% of the time
where the time goes in v4:
time: 33.2 us; the launch traced here: 33.1 us
  Pallas kernels  33.1 us (100%)
    pallas_call x1, Pallas kernels, gather(): pl.pallas_call(gather_kernel, out_shape=[jax.ShapeDtypeStruct((512, 256),...  31.2 us
    pallas_call x1, Pallas kernels, update(): pl.pallas_call(update_kernel, out_shape=jax.ShapeDtypeStruct((512, 1024),...  1.84 us

profile of v4, /device:TPU:1, one launch (start us, length us, event | category | flops | bytes accessed | tf_op | source)
XLA Modules:
  0.0 33.1 jit_solution(3146973907735557740)
XLA Ops:
  0.0 31.2 %gather_panel.1 = (bf16[512,256]{1,0:T(8,128)(2,1)S(1)}, bf16[512,256]{1,0:T(8,128)(2,1)S(1)}, bf16[256,1024]{1,0:T(8,128)(2,1)S(1)}, bf16[256,1024]{1,0:T(8,128)(2,1)S(1)}, f32[512,1024]{1,0:T(8,128)S(1)}) custom-call(f32[16,512]{1,0:T(8,128)} %bitcast.1, f32[256,256]{1,0:T(8,128)} %lower_ref.1, f32[512,1024]{1,0:T(8,128)} %trailing_ref.1), custom_call_target="tpu_custom_call" | custom-call | tf_op jit(solution)/shard_map/gather_panel/pallas_call | solution.py:250
  31.2 1.8 %update.1 = f32[512,1024]{1,0:T(8,128)} custom-call(bf16[512,256]{1,0:T(8,128)(2,1)S(1)} %get-tuple-element.10.g_high, bf16[512,256]{1,0:T(8,128)(2,1)S(1)} %get-tuple-element.11.g_low, bf16[256,1024]{1,0:T(8,128)(2,1)S(1)} %get-tuple-element.12.c_high, bf16[256,1024]{1,0:T(8,128)(2,1)S(1)} %get-tuple-element.13.c_low, ...), custom_call_target="tpu_custom_call" | custom-call | tf_op jit(solution)/shard_map/update/pallas_call | solution.py:287

commit v5 on v4

--- a/solution.py
+++ b/solution.py
@@ -40,7 +40,7 @@
     slice_ref, lower_ref, trailing_ref,
     g_high, g_low, c_high, c_low, near_trailing,
     rows, cols, lower, relay,
-    near_sem, layer_sem, local_sem, row_send, row_recv, relay_recv, hold_sem, cast_send, cast_recv, pass_send, pass_recv,
+    hello_sem, near_sem, layer_sem, local_sem, row_send, row_recv, relay_recv, hold_sem, cast_send, cast_recv, pass_send, pass_recv,
 ):
     me, z = lax.axis_index("row"), lax.axis_index("col")
     core, x, y = me % 2, (me // 2) % SIDE, me // (2 * SIDE)
@@ -62,18 +62,17 @@
 
     @pl.when(core == 1)
     def _():
-        for delta in (3, -3):
-            tell(barrier, (me - 1, above(delta)[1]))
         for partner in [above(delta) for delta in NEAR] + across + along:
             tell(barrier, partner)
 
-    goal = me % LAYERS
-    climb = (goal - z + LAYERS) % LAYERS
-    spot = lookup(HOLDER, climb)
-    goal_core = jnp.where((climb >= 4) & (climb < 12), 1, 0)
-    goal_place = spot + 2 * SIDE * (me // LAYERS)
-    goal_y, goal_x = (y + spot // SIDE) % SIDE, (x + spot % SIDE) % SIDE
-    holder = ((goal_y * SIDE + goal_x) * 2 + goal_core, goal)
+    def target(row):
+        climb = (row % LAYERS - z + LAYERS) % LAYERS
+        spot = lookup(HOLDER, climb)
+        to_core = jnp.where((climb >= 4) & (climb < 12), 1, 0)
+        to_y, to_x = (y + spot // SIDE) % SIDE, (x + spot % SIDE) % SIDE
+        there = ((to_y * SIDE + to_x) * 2 + to_core, row % LAYERS)
+        return to_core, spot + 2 * SIDE * (row // LAYERS), there
+
     owner_y, owner_x = z // (2 * SIDE), (z // 2) % SIDE
 
     def place_of(dy, dx):
@@ -81,7 +80,7 @@
 
     place = place_of(0, 0)
     risen = jnp.where(core == 1, lookup(CLIMB[1], place % 8), lookup(CLIMB[0], place % 8))
-    giver = (z + LAYERS * (place // 8), (z - risen + LAYERS) % LAYERS)
+    giver = (z // 2 * 2 + LAYERS * (place // 8), (z - risen + LAYERS) % LAYERS)
 
     tell(barrier, giver)
     own = pltpu.make_async_copy(slice_ref, rows.at[z], local_sem.at[0])
@@ -91,7 +90,6 @@
     keep = pltpu.make_async_copy(trailing_ref, near_trailing, local_sem.at[2])
     keep.start()
     own.wait()
-    pl.semaphore_wait(barrier, jnp.where(core == 0, 4, 14))
 
     def send(src, dst, send_sem, recv_sem, device):
         pltpu.make_async_remote_copy(
@@ -123,26 +121,43 @@
     def row_wait(offset):
         wait(row_slot(offset), row_recv.at[RELAYED[offset]])
 
-    def to_holder():
-        send(rows.at[z], cols.at[goal_core, goal_place], hold_sem.at[0], hold_sem.at[1], holder)
-
-    pl.when(core == 0)(to_holder)
+    soon = me % LAYERS < LAYERS // 2
 
     @pl.when(core == 0)
     def _():
+        own_core, own_place, own_holder = target(me)
+        next_core, next_place, next_holder = target(me + 1)
+
+        def to_holders():
+            pl.semaphore_wait(barrier, 3)
+            pl.when(soon)(lambda: tell(hello_sem, sibling))
+            send(rows.at[z], cols.at[own_core, own_place], hold_sem.at[0], hold_sem.at[1], own_holder)
+            wait(relay.at[0], relay_recv.at[0])
+            send(relay.at[0], cols.at[next_core, next_place], hold_sem.at[2], hold_sem.at[1], next_holder)
+
+        pl.when(soon)(to_holders)
+        pl.semaphore_wait(near_sem, 1)
         for delta in (3, -3):
             index = RELAYED[-delta]
             there = (me + 1, (z + delta + LAYERS) % LAYERS)
             send(rows.at[z], relay.at[index], row_send.at[0], relay_recv.at[index], there)
-
-    @pl.when(core == 1)
-    def _():
+        pl.when(jnp.logical_not(soon))(to_holders)
+
+    @pl.when(core == 1)
+    def _():
+        def to_sibling():
+            send(rows.at[z], relay.at[0], hold_sem.at[0], relay_recv.at[0], sibling)
+
+        @pl.when(soon)
+        def _():
+            pl.semaphore_wait(hello_sem, 1)
+            to_sibling()
+
+        pl.semaphore_wait(barrier, 13)
+        tell(near_sem, sibling)
+        pl.when(jnp.logical_not(soon))(to_sibling)
         row_copy(0, 3)
         row_copy(0, -3)
-        to_holder()
-
-    @pl.when(core == 1)
-    def _():
         for partner in along + [above(delta) for delta in (1, -1, 2, -2)]:
             tell(near_sem, partner)
 
@@ -236,6 +251,7 @@
         wait(rows.at[pl.ds(0, 15)], row_send.at[1])
 
     wait(rows.at[z], hold_sem.at[0])
+    pl.when(core == 0)(lambda: wait(relay.at[0], hold_sem.at[2]))
     wait(cols.at[core, pl.ds(0, 15)], cast_send)
     wait(cols.at[core], pass_send)
     for batch in BATCHES:
@@ -259,7 +275,7 @@
             pltpu.VMEM((2, LAYERS, 16, 512), jnp.float32),
             pltpu.VMEM((256, 256), jnp.float32),
             pltpu.VMEM((4, 16, 512), jnp.float32),
-            pltpu.SemaphoreType.REGULAR, pltpu.SemaphoreType.REGULAR, dma((3,)), dma((2,)), dma((5,)), dma((4,)), dma((2,)),
+            *[pltpu.SemaphoreType.REGULAR] * 3, dma((3,)), dma((2,)), dma((5,)), dma((4,)), dma((3,)),
             dma, dma((4,)), dma, dma((4,)),
         ],
         compiler_params=pltpu.CompilerParams(

time: 33.2 us -> 32.9 us (level)
  the two profiles are of different devices: /device:TPU:1 before, /device:TPU:4 now
where the time goes in v5:
time: 32.9 us; the launch traced here: 32.8 us
  Pallas kernels  32.8 us (100%)
    pallas_call x1, Pallas kernels, gather(): pl.pallas_call(gather_kernel, out_shape=[jax.ShapeDtypeStruct((512, 256),...  30.9 us
    pallas_call x1, Pallas kernels, update(): pl.pallas_call(update_kernel, out_shape=jax.ShapeDtypeStruct((512, 1024),...  1.84 us

profile of v5, /device:TPU:4, one launch (start us, length us, event | category | flops | bytes accessed | tf_op | source)
XLA Modules:
  0.0 32.8 jit_solution(15724554636149235837)
XLA Ops:
  0.0 30.9 %gather_panel.1 = (bf16[512,256]{1,0:T(8,128)(2,1)S(1)}, bf16[512,256]{1,0:T(8,128)(2,1)S(1)}, bf16[256,1024]{1,0:T(8,128)(2,1)S(1)}, bf16[256,1024]{1,0:T(8,128)(2,1)S(1)}, f32[512,1024]{1,0:T(8,128)S(1)}) custom-call(f32[16,512]{1,0:T(8,128)} %bitcast.1, f32[256,256]{1,0:T(8,128)} %lower_ref.1, f32[512,1024]{1,0:T(8,128)} %trailing_ref.1), custom_call_target="tpu_custom_call" | custom-call | tf_op jit(solution)/shard_map/gather_panel/pallas_call | solution.py:266
  30.9 1.8 %update.1 = f32[512,1024]{1,0:T(8,128)} custom-call(bf16[512,256]{1,0:T(8,128)(2,1)S(1)} %get-tuple-element.10.g_high, bf16[512,256]{1,0:T(8,128)(2,1)S(1)} %get-tuple-element.11.g_low, bf16[256,1024]{1,0:T(8,128)(2,1)S(1)} %get-tuple-element.12.c_high, bf16[256,1024]{1,0:T(8,128)(2,1)S(1)} %get-tuple-element.13.c_low, ...), custom_call_target="tpu_custom_call" | custom-call | tf_op jit(solution)/shard_map/update/pallas_call | solution.py:303

commit v6 on v5

--- a/solution.py
+++ b/solution.py
@@ -9,6 +9,7 @@
 
 MESH = pl.DeviceIdType.MESH
 LAYERS = 16
+LATE_LAYERS = 8
 SIDE = 4
 FAR = {8: (0, 0), 7: (0, 1), 9: (0, 3), 6: (1, 0), 10: (0, 2), 5: (1, 1), 11: (1, 3), 4: (1, 2)}
 CLOSE = {12: (0, 0), 3: (0, 1), 13: (0, 3), 2: (1, 0), 14: (0, 2), 1: (1, 1), 15: (1, 3), 0: (1, 2)}
@@ -189,15 +190,7 @@
                 guest_copy(-3 * way, delta)
 
     pl.when(core == 0)(lambda: pl.semaphore_wait(layer_sem, 1))
-    held = cols.at[core, place]
-    wait(held, hold_sem.at[1])
-    for other in OTHERS[::-1]:
-        send(held, held, cast_send, cast_recv.at[place // BATCH], beside(*other))
-    row_copy(0, 1)
-    row_copy(0, -1)
-
-    @pl.when(core == 1)
-    def _():
+    def relay_last():
         for way in (1, -1):
             row_wait(-6 * way)
             row_copy(-6 * way, 2 * way, 0 if way > 0 else 1)
@@ -208,6 +201,17 @@
             guest_copy(-6 * way, 2 * way, 0 if way > 0 else 1)
             for delta in (way, -way, 0):
                 guest_copy(-6 * way, delta)
+
+    relay_first = (z >= LATE_LAYERS) & (me % LAYERS >= 2)
+    pl.when((core == 1) & relay_first)(relay_last)
+    row_copy(0, 1)
+    row_copy(0, -1)
+    held = cols.at[core, place]
+    wait(held, hold_sem.at[1])
+    for other in OTHERS[::-1]:
+        send(held, held, cast_send, cast_recv.at[place // BATCH], beside(*other))
+
+    pl.when((core == 1) & jnp.logical_not(relay_first))(relay_last)
 
     def store(holding, batch):
         for there in range(BATCH * batch, BATCH * (batch + 1)):

time: 32.9 us -> 31.6 us (0.960)
  the two profiles are of different devices: /device:TPU:4 before, /device:TPU:1 now
where the time goes in v6:
time: 31.6 us; the launch traced here: 31.4 us
  Pallas kernels  31.4 us (99%)
    pallas_call x1, Pallas kernels, gather(): pl.pallas_call(gather_kernel, out_shape=[jax.ShapeDtypeStruct((512, 256),...  29.6 us
    pallas_call x1, Pallas kernels, update(): pl.pallas_call(update_kernel, out_shape=jax.ShapeDtypeStruct((512, 1024),...  1.83 us

profile of v6, /device:TPU:1, one launch (start us, length us, event | category | flops | bytes accessed | tf_op | source)
XLA Modules:
  0.0 31.4 jit_solution(18384024467326650993)
XLA Ops:
  0.0 29.6 %gather_panel.1 = (bf16[512,256]{1,0:T(8,128)(2,1)S(1)}, bf16[512,256]{1,0:T(8,128)(2,1)S(1)}, bf16[256,1024]{1,0:T(8,128)(2,1)S(1)}, bf16[256,1024]{1,0:T(8,128)(2,1)S(1)}, f32[512,1024]{1,0:T(8,128)S(1)}) custom-call(f32[16,512]{1,0:T(8,128)} %bitcast.1, f32[256,256]{1,0:T(8,128)} %lower_ref.1, f32[512,1024]{1,0:T(8,128)} %trailing_ref.1), custom_call_target="tpu_custom_call" | custom-call | tf_op jit(solution)/shard_map/gather_panel/pallas_call | solution.py:270
  29.6 1.8 %update.1 = f32[512,1024]{1,0:T(8,128)} custom-call(bf16[512,256]{1,0:T(8,128)(2,1)S(1)} %get-tuple-element.10.g_high, bf16[512,256]{1,0:T(8,128)(2,1)S(1)} %get-tuple-element.11.g_low, bf16[256,1024]{1,0:T(8,128)(2,1)S(1)} %get-tuple-element.12.c_high, bf16[256,1024]{1,0:T(8,128)(2,1)S(1)} %get-tuple-element.13.c_low, ...), custom_call_target="tpu_custom_call" | custom-call | tf_op jit(solution)/shard_map/update/pallas_call | solution.py:307

commit v7 on v6

--- a/solution.py
+++ b/solution.py
@@ -202,7 +202,7 @@
             for delta in (way, -way, 0):
                 guest_copy(-6 * way, delta)
 
-    relay_first = (z >= LATE_LAYERS) & (me % LAYERS >= 2)
+    relay_first = (z >= LATE_LAYERS) & (x > 0)
     pl.when((core == 1) & relay_first)(relay_last)
     row_copy(0, 1)
     row_copy(0, -1)

time: 31.6 us -> 31.6 us (level)
  no operation moved by 1% of the time
where the time goes in v7:
time: 31.6 us; the launch traced here: 31.4 us
  Pallas kernels  31.4 us (99%)
    pallas_call x1, Pallas kernels, gather(): pl.pallas_call(gather_kernel, out_shape=[jax.ShapeDtypeStruct((512, 256),...  29.6 us
    pallas_call x1, Pallas kernels, update(): pl.pallas_call(update_kernel, out_shape=jax.ShapeDtypeStruct((512, 1024),...  1.83 us

profile of v7, /device:TPU:1, one launch (start us, length us, event | category | flops | bytes accessed | tf_op | source)
XLA Modules:
  0.0 31.4 jit_solution(7853885353978168259)
XLA Ops:
  0.0 29.6 %gather_panel.1 = (bf16[512,256]{1,0:T(8,128)(2,1)S(1)}, bf16[512,256]{1,0:T(8,128)(2,1)S(1)}, bf16[256,1024]{1,0:T(8,128)(2,1)S(1)}, bf16[256,1024]{1,0:T(8,128)(2,1)S(1)}, f32[512,1024]{1,0:T(8,128)S(1)}) custom-call(f32[16,512]{1,0:T(8,128)} %bitcast.1, f32[256,256]{1,0:T(8,128)} %lower_ref.1, f32[512,1024]{1,0:T(8,128)} %trailing_ref.1), custom_call_target="tpu_custom_call" | custom-call | tf_op jit(solution)/shard_map/gather_panel/pallas_call | solution.py:270
  29.6 1.8 %update.1 = f32[512,1024]{1,0:T(8,128)} custom-call(bf16[512,256]{1,0:T(8,128)(2,1)S(1)} %get-tuple-element.10.g_high, bf16[512,256]{1,0:T(8,128)(2,1)S(1)} %get-tuple-element.11.g_low, bf16[256,1024]{1,0:T(8,128)(2,1)S(1)} %get-tuple-element.12.c_high, bf16[256,1024]{1,0:T(8,128)(2,1)S(1)} %get-tuple-element.13.c_low, ...), custom_call_target="tpu_custom_call" | custom-call | tf_op jit(solution)/shard_map/update/pallas_call | solution.py:307
